TPU v7x, 32 devices: a whole 2x2x4 slice. The times are simulated.
32 devices in a mesh: row: 8 (over z, y), col: 4 (over x, core).
Axes of the slice: x: 2, y: 2, z: 4, core: 2. Of those that a mesh axis runs over, the one named last changes fastest.
Arguments:
- token_acts: bfloat16 [4, 1024, 768], P('col', 'row'), may hold values from -6 to 6
- pair_feats: bfloat16 [1024, 1024, 128], P('row', 'col'), may hold values from -6 to 6
- pair_mask: int32 [1024, 1024], P('row', 'col'), may hold values 0 or 1
- norm_gain: float32 [768], replicated, may hold values from 0.1 to 1.9
- norm_shift: float32 [768], replicated, may hold values from -3 to 3
- w_query: bfloat16 [768, 768], replicated, may hold values from -0.21875 to 0.21875
- query_bias: float32 [768], replicated, may hold values from -3 to 3
- w_key: bfloat16 [768, 768], replicated, may hold values from -0.21875 to 0.21875
- w_value: bfloat16 [768, 768], replicated, may hold values from -0.21875 to 0.21875
- w_gate: bfloat16 [768, 768], replicated, may hold values from -0.21875 to 0.21875
- w_out: bfloat16 [768, 768], replicated, may hold values from -0.21875 to 0.21875
- pair_gain: float32 [128], replicated, may hold values from 0.1 to 1.9
- w_pair: bfloat16 [128, 16], replicated, may hold values from -16 to 16, as said below
- grad_out: bfloat16 [4, 1024, 768], P('col', 'row'), may hold values from -6 to 6
Outputs:
- block_out: bfloat16 [4, 1024, 768], P('col', 'row')
- grad_acts: bfloat16 [4, 1024, 768], P('col', 'row')
- grad_pair: bfloat16 [1024, 1024, 128], P('row', 'col')
Inputs may be any that keep to these rules, and one draw needn't show every extreme that they name: `w_pair`: entries of either sign.
All inputs are finite; a program needn't handle non-finite values. No bound on the sum of `pair_mask` on one device may be relied on, other than what follows from the above.
Results may differ from a plain program's by a relative error of at most 0.011.
The roundings to bfloat16 on the way count: a program that leaves them out, or rounds other values in their place, can miss the bound.
Values may be sent and summed in bfloat16 or wider, within the bound.
A program may use at most 192 MiB of HBM per device.

v0:
```python
import functools
import math

import jax
import jax.numpy as jnp
from jax import lax
from jax.experimental import pallas as pl
from jax.experimental.pallas import tpu as pltpu
from jax.sharding import PartitionSpec as P

epsilon = 1e-05
highest = lax.Precision.HIGHEST


def normalize(inputs):
    row_mean = jnp.mean(inputs, axis=-1, keepdims=True)
    centred = inputs - row_mean
    variance = jnp.mean(centred * centred, axis=-1, keepdims=True)
    inv_std = lax.rsqrt(variance + epsilon)
    return (centred * inv_std, inv_std)


def norm_backward(standard, inv_std, gain_vec, upstream):
    scaled = upstream * gain_vec
    grad_mean = jnp.mean(scaled, axis=-1, keepdims=True)
    cross_mean = jnp.mean(scaled * standard, axis=-1, keepdims=True)
    return (scaled - grad_mean - standard * cross_mean) * inv_std


def back_project(upstream, matrix):
    return jnp.einsum("io,do->id", upstream, matrix.astype(jnp.float32), precision=highest)


def place():
    row, col = lax.axis_index("row"), lax.axis_index("col")
    return row // 2, row % 2, col // 2, col % 2


def peer(line=None, side=None, chip=None, core=None):
    own = place()
    line, side, chip, core = (
        mine if given is None else given for mine, given in zip(own, (line, side, chip, core))
    )
    return (line * 2 + side, chip * 2 + core)


def remote(source, target, send_sem, recv_sem, device):
    return pltpu.make_async_remote_copy(
        src_ref=source,
        dst_ref=target,
        send_sem=send_sem,
        recv_sem=recv_sem,
        device_id=device,
        device_id_type=pl.DeviceIdType.MESH,
    )


def greet(lines, chips):
    line, side, chip, core = place()
    barrier = pltpu.get_barrier_semaphore()
    others = [peer(side=1 - side), peer(core=1 - core)]
    others += [peer(line=(line + 1) % lines), peer(line=(line + lines - 1) % lines)]
    others += [peer(chip=(chip + step) % chips) for step in range(1, chips)]
    for other in others:
        pl.semaphore_signal(barrier, inc=1, device_id=other, device_id_type=pl.DeviceIdType.MESH)
    pl.semaphore_wait(barrier, len(others))


def gather_kernel(
    lines, chips, kv, tile, kv_all, bias_all,
    local_sem, up_send, down_send, side_send, line_recv, side_recv,
    chip_send, chip_recv, core_send, core_recv,
):
    line, side, chip, core = place()
    width = tile.shape[2]
    greet(lines, chips)

    def slot(which_line, which_side):
        return kv_all.at[which_line * 2 + which_side]

    def columns(which_chip, which_core):
        start = pl.multiple_of((which_chip * 2 + which_core) * width, width)
        return bias_all.at[:, :, pl.ds(start, width)]

    sends = []
    for step in range(1, chips):
        sends.append(remote(
            tile, columns(chip, core), chip_send.at[step], chip_recv.at[step],
            peer(chip=(chip + step) % chips),
        ))
    sends.append(remote(
        tile, columns(chip, core), core_send.at[0], core_recv.at[0], peer(core=1 - core)
    ))
    for copy in sends:
        copy.start()

    def upward(source, origin):
        return remote(
            source, slot(origin, side), up_send.at[origin], line_recv.at[origin],
            peer(line=jnp.minimum(line + 1, lines - 1)),
        )

    def downward(source, origin):
        return remote(
            source, slot(origin, side), down_send.at[origin], line_recv.at[origin],
            peer(line=jnp.maximum(line - 1, 0)),
        )

    def sideward(source, origin):
        return remote(
            source, slot(origin, side), side_send.at[origin], side_recv.at[origin],
            peer(side=1 - side),
        )

    @pl.when(line < lines - 1)
    def _():
        upward(kv, line).start()

    @pl.when(line > 0)
    def _():
        downward(kv, line).start()

    sideward(kv, line).start()
    keep_kv = pltpu.make_async_copy(kv, slot(line, side), local_sem.at[0])
    keep_tile = pltpu.make_async_copy(tile, columns(chip, core), local_sem.at[1])
    keep_kv.start()
    keep_tile.start()

    for step in range(1, lines):
        @pl.when(line - step >= 0)
        def _():
            origin = line - step
            upward(slot(origin, side), origin).wait_recv()

            @pl.when(line < lines - 1)
            def _():
                upward(slot(origin, side), origin).start()

            sideward(slot(origin, side), origin).start()

        @pl.when(line + step < lines)
        def _():
            origin = line + step
            downward(slot(origin, side), origin).wait_recv()

            @pl.when(line > 0)
            def _():
                downward(slot(origin, side), origin).start()

            sideward(slot(origin, side), origin).start()

    for step in range(1, chips):
        origin = (chip + chips - step) % chips
        block = columns(origin, core)
        remote(tile, block, chip_send.at[step], chip_recv.at[step], peer(core=1 - core)).wait_recv()
        copy = remote(block, block, core_send.at[step], core_recv.at[step], peer(core=1 - core))
        copy.start()
        sends.append(copy)
    for step in range(chips):
        origin = (chip + chips - step) % chips
        block = columns(origin, 1 - core)
        remote(tile, block, core_send.at[step], core_recv.at[step], peer(core=1 - core)).wait_recv()
    for origin in range(lines):
        block = slot(origin, 1 - side)
        remote(
            kv, block, side_send.at[origin], side_recv.at[origin], peer(side=1 - side)
        ).wait_recv()
    for copy in sends:
        copy.wait_send()
    for origin in range(lines):
        sideward(kv, origin).wait_send()

        @pl.when((line < lines - 1) & (origin <= line))
        def _():
            upward(kv, origin).wait_send()

        @pl.when((line > 0) & (origin >= line))
        def _():
            downward(kv, origin).wait_send()

    keep_kv.wait()
    keep_tile.wait()


def gather(kv, tile, rows, cols):
    lines, chips = rows // 2, cols // 2
    heads, height, width = tile.shape
    anywhere = pl.BlockSpec(memory_space=pl.ANY)
    dma = pltpu.SemaphoreType.DMA
    return pl.pallas_call(
        functools.partial(gather_kernel, lines, chips),
        out_shape=(
            jax.ShapeDtypeStruct((rows,) + kv.shape, kv.dtype),
            jax.ShapeDtypeStruct((heads, height, width * cols), tile.dtype),
        ),
        in_specs=[anywhere] * 2,
        out_specs=(anywhere, anywhere),
        scratch_shapes=[
            dma((2,)), dma((lines,)), dma((lines,)), dma((lines,)), dma((lines,)), dma((lines,)),
            dma((chips,)), dma((chips,)), dma((chips,)), dma((chips,)),
        ],
        compiler_params=pltpu.CompilerParams(
            collective_id=0, has_side_effects=True, vmem_limit_bytes=48 * 2**20
        ),
    )(kv, tile)


def reduce_kernel(
    lines, chips, dkv, ds, kv_sum, ds_sum,
    side_in, line_out, up_in, down_in, core_in, chip_out, chip_in,
    side_send, side_recv, line_send, up_recv, down_recv,
    core_send, core_recv, chip_send, chip_recv,
):
    line, side, chip, core = place()
    heads, height, width = ds_sum.shape
    depth = kv_sum.shape[0]
    greet(lines, chips)

    def columns(which_chip, which_core):
        start = pl.multiple_of((which_chip * 2 + which_core) * width, width)
        return pl.ds(start, width)

    sends = []
    for step in [*range(1, chips), 0]:
        copy = remote(
            ds.at[:, :, columns((chip + step) % chips, 1 - core)], core_in.at[step],
            core_send.at[step], core_recv.at[step], peer(core=1 - core),
        )
        copy.start()
        sends.append(copy)
    order = []
    for step in range(lines):
        for item in (lines - 1 - step, step):
            if item not in order:
                order.append(item)
    for item in order:
        copy = remote(
            dkv.at[item * 2 + 1 - side], side_in.at[item], side_send.at[item],
            side_recv.at[item], peer(side=1 - side),
        )
        copy.start()
        sends.append(copy)
    for step in range(1, chips):
        other = (chip + step) % chips
        sends[step - 1].wait_recv()

        @pl.loop(0, heads)
        def _(head):
            mine = ds[head, :, columns(other, core)].astype(jnp.float32)
            total = mine + core_in[step, head].astype(jnp.float32)
            chip_out[step, head] = total.astype(chip_out.dtype)

        copy = remote(
            chip_out.at[step], chip_in.at[step], chip_send.at[step], chip_recv.at[step],
            peer(chip=other),
        )
        copy.start()
        sends.append(copy)

    chunk = 16

    def pieces(write):
        @pl.loop(0, depth // chunk)
        def _(piece):
            write(pl.ds(pl.multiple_of(piece * chunk, chunk), chunk))

    def pair(target, part):
        mine = dkv[target * 2 + side, part, :].astype(jnp.float32)
        return mine + side_in[target, part, :].astype(jnp.float32)

    def side_wait(target):
        remote(
            dkv.at[0], side_in.at[target], side_send.at[target], side_recv.at[target],
            peer(side=1 - side),
        ).wait_recv()

    def upward(target):
        return remote(
            line_out.at[target], up_in.at[target], line_send.at[target], up_recv.at[target],
            peer(line=jnp.minimum(line + 1, lines - 1)),
        )

    def downward(target):
        return remote(
            line_out.at[target], down_in.at[target], line_send.at[target], down_recv.at[target],
            peer(line=jnp.maximum(line - 1, 0)),
        )

    def pass_on(target, make, arrived, first):
        side_wait(target)

        @pl.when(first)
        def _():
            def write(part):
                line_out[target, part, :] = pair(target, part).astype(line_out.dtype)

            pieces(write)

        @pl.when(jnp.logical_not(first))
        def _():
            make(target).wait_recv()

            def write(part):
                total = pair(target, part) + arrived[target, part, :].astype(jnp.float32)
                line_out[target, part, :] = total.astype(line_out.dtype)

            pieces(write)

        make(target).start()

    for step in range(lines - 1):
        top = lines - 1 - step

        @pl.when(line < top)
        def _():
            pass_on(top, upward, up_in, line == 0)

        @pl.when(line > step)
        def _():
            pass_on(step, downward, down_in, line == lines - 1)

    side_wait(line)

    def write_pair(part):
        kv_sum[part, :] = pair(line, part)

    pieces(write_pair)

    @pl.when(line > 0)
    def _():
        upward(line).wait_recv()

        def write(part):
            kv_sum[part, :] += up_in[line, part, :].astype(jnp.float32)

        pieces(write)

    @pl.when(line < lines - 1)
    def _():
        downward(line).wait_recv()

        def write(part):
            kv_sum[part, :] += down_in[line, part, :].astype(jnp.float32)

        pieces(write)

    sends[chips - 1].wait_recv()
    for step in range(1, chips):
        remote(
            chip_out.at[step], chip_in.at[step], chip_send.at[step], chip_recv.at[step],
            peer(core=1 - core),
        ).wait_recv()

    @pl.loop(0, heads)
    def _(head):
        total = ds[head, :, columns(chip, core)].astype(jnp.float32)
        total += core_in[0, head].astype(jnp.float32)
        for step in range(1, chips):
            total += chip_in[step, head].astype(jnp.float32)
        ds_sum[head] = total.astype(ds_sum.dtype)

    for copy in sends:
        copy.wait_send()
    for target in range(lines):
        @pl.when(line != target)
        def _():
            upward(target).wait_send()


def reduce(dkv, ds, rows, cols):
    lines, chips = rows // 2, cols // 2
    heads, height, width = ds.shape
    width //= cols
    depth, wide = dkv.shape[0] // rows, dkv.shape[1]
    inside = pl.BlockSpec(memory_space=pltpu.VMEM)
    dma = pltpu.SemaphoreType.DMA
    half = jnp.bfloat16
    return pl.pallas_call(
        functools.partial(reduce_kernel, lines, chips),
        out_shape=(
            jax.ShapeDtypeStruct((depth, wide), jnp.float32),
            jax.ShapeDtypeStruct((heads, height, width), jnp.float32),
        ),
        in_specs=[inside] * 2,
        out_specs=(inside, inside),
        scratch_shapes=[
            *[pltpu.VMEM((lines, depth, wide), half)] * 4,
            *[pltpu.VMEM((chips, heads, height, width), half)] * 3,
            *[dma((lines,))] * 5,
            *[dma((chips,))] * 4,
        ],
        compiler_params=pltpu.CompilerParams(
            collective_id=1, has_side_effects=True, vmem_limit_bytes=52 * 2**20
        ),
    )(dkv.reshape(rows, depth, wide), ds)


def lane_mean(values, ones):
    high = values.astype(jnp.bfloat16)
    low = (values - high.astype(jnp.float32)).astype(jnp.bfloat16)
    return jnp.dot(
        jnp.concatenate([high, low], axis=1), ones, preferred_element_type=jnp.float32
    )


def pair_standard(feats, centre, ones):
    centred = jnp.dot(feats, centre, preferred_element_type=jnp.float32)
    inv_std = lax.rsqrt(lane_mean(centred * centred, ones) + epsilon)
    return centred * inv_std, inv_std


def pair_forward_kernel(feats, centre, ones, gain, weights, out):
    for item in range(feats.shape[0]):
        standard, _ = pair_standard(feats[item], centre[...], ones[...])
        normed = (standard * gain[...]).astype(jnp.bfloat16)
        out[item] = lax.dot_general(
            weights[...], normed, (((1,), (1,)), ((), ())), preferred_element_type=jnp.float32
        ).astype(jnp.bfloat16)


def pair_backward_kernel(feats, centre, ones, bias_grad, weights, out):
    for item in range(feats.shape[0]):
        standard, inv_std = pair_standard(feats[item], centre[...], ones[...])
        grad = bias_grad[item]
        high = grad.astype(jnp.bfloat16).astype(jnp.float32)
        low = grad - high
        parts = jnp.concatenate([high, low, high, low], axis=0).T.astype(jnp.bfloat16)
        scaled = jnp.dot(parts, weights[...], preferred_element_type=jnp.float32)
        cross_mean = lane_mean(scaled * standard, ones[...])
        out[item] = ((scaled - standard * cross_mean) * inv_std).astype(jnp.bfloat16)


def pair_call(kernel, pair_feats, extra, extra_specs, out_shape, block=8):
    rows, width, channels = pair_feats.shape
    eye = jnp.eye(channels, dtype=jnp.float32)
    centre = (eye - 1.0 / channels).astype(jnp.bfloat16)
    ones = jnp.full((2 * channels, channels), 1.0 / channels, jnp.bfloat16)
    whole = lambda shape: pl.BlockSpec(shape, lambda step: (0,) * len(shape))
    tiled = lambda shape: pl.BlockSpec((block,) + shape[1:], lambda step: (step, 0, 0))
    return pl.pallas_call(
        kernel,
        grid=(rows // block,),
        out_shape=jax.ShapeDtypeStruct(out_shape, jnp.bfloat16),
        in_specs=[
            tiled(pair_feats.shape), whole(centre.shape), whole(ones.shape),
            *[(tiled if spec else whole)(item.shape) for item, spec in zip(extra, extra_specs)],
        ],
        out_specs=tiled(out_shape),
        compiler_params=pltpu.CompilerParams(vmem_limit_bytes=32 * 2**20),
    )(pair_feats, centre, ones, *extra)


def pair_forward(pair_feats, pair_gain, w_pair):
    rows, width, channels = pair_feats.shape
    return pair_call(
        pair_forward_kernel, pair_feats, (pair_gain[None], w_pair.T), (False, False),
        (rows, w_pair.shape[1], width),
    )


def pair_backward(pair_feats, pair_gain, w_pair, bias_grad):
    scaled = w_pair.astype(jnp.float32).T * pair_gain
    scaled = scaled - jnp.mean(scaled, axis=1, keepdims=True)
    high = lax.reduce_precision(scaled, 8, 7)
    low = scaled - high
    weights = jnp.concatenate([high, high, low, low], axis=0).astype(jnp.bfloat16)
    return pair_call(
        pair_backward_kernel, pair_feats, (jnp.transpose(bias_grad, (1, 0, 2)), weights),
        (True, False), pair_feats.shape,
    )


def body(
    rows,
    cols,
    token_acts,
    pair_feats,
    pair_mask,
    norm_gain,
    norm_shift,
    w_query,
    query_bias,
    w_key,
    w_value,
    w_gate,
    w_out,
    pair_gain,
    w_pair,
    grad_out,
):
    row_count = token_acts.shape[1]
    model_width = token_acts.shape[2]
    col_count = pair_feats.shape[1]
    head_count = w_pair.shape[1]
    head_size = model_width // head_count
    score_scale = 1.0 / math.sqrt(head_size)
    row_start = lax.axis_index("row") * row_count
    col_start = lax.axis_index("col") * col_count
    pair_bias = jnp.transpose(pair_forward(pair_feats, pair_gain, w_pair), (1, 0, 2))
    row_index = row_start + lax.broadcasted_iota(jnp.int32, (row_count, col_count), 0)
    col_index = col_start + lax.broadcasted_iota(jnp.int32, (row_count, col_count), 1)
    allowed = (pair_mask == 1) | (row_index == col_index)
    biased = jnp.where(allowed[None], pair_bias, jnp.bfloat16(-1000000000.0))
    standard, inv_std = normalize(token_acts[0].astype(jnp.float32))
    normed = (standard * norm_gain + norm_shift).astype(jnp.bfloat16)
    query = (jnp.dot(normed, w_query, preferred_element_type=jnp.float32) + query_bias).astype(
        jnp.bfloat16
    )
    gate_open = jax.nn.sigmoid(jnp.dot(normed, w_gate, preferred_element_type=jnp.float32))
    own_keys = jnp.dot(normed, w_key, preferred_element_type=jnp.float32).astype(jnp.bfloat16)
    own_values = jnp.dot(normed, w_value, preferred_element_type=jnp.float32).astype(jnp.bfloat16)
    both, bias_full = gather(jnp.concatenate([own_keys, own_values], axis=1), biased, rows, cols)
    both = both.reshape(rows * row_count, 2 * model_width)
    all_keys, all_values = both[:, :model_width], both[:, model_width:]
    key_count = all_keys.shape[0]
    query_heads = query.reshape(row_count, head_count, head_size)
    key_heads = all_keys.reshape(key_count, head_count, head_size)
    value_heads = all_values.reshape(key_count, head_count, head_size)
    scores = jnp.einsum(
        "ihe,jhe->hij", query_heads, key_heads, preferred_element_type=jnp.float32
    ) * score_scale + bias_full.astype(jnp.float32)
    attn_probs = jax.nn.softmax(scores, axis=-1)
    probs_b = attn_probs.astype(jnp.bfloat16)
    attended = jnp.einsum(
        "hij,jhe->ihe", probs_b, value_heads, preferred_element_type=jnp.float32
    ).reshape(row_count, model_width)
    gated_out = (gate_open * attended).astype(jnp.bfloat16)
    block_out = jnp.dot(gated_out, w_out, preferred_element_type=jnp.float32).astype(jnp.bfloat16)
    d_gated = jnp.einsum("io,do->id", grad_out[0], w_out, preferred_element_type=jnp.float32)
    d_att = (d_gated * gate_open).astype(jnp.bfloat16)
    d_gate_pre = d_gated * attended * gate_open * (1.0 - gate_open)
    att_heads = d_att.reshape(row_count, head_count, head_size)
    d_probs = jnp.einsum("ihe,jhe->hij", att_heads, value_heads, preferred_element_type=jnp.float32)
    row_delta = jnp.sum(attn_probs * d_probs, axis=-1, keepdims=True)
    d_scores = attn_probs * (d_probs - row_delta)
    ds_b = d_scores.astype(jnp.bfloat16)
    d_query = (
        jnp.einsum("hij,jhe->ihe", ds_b, key_heads, preferred_element_type=jnp.float32)
        * score_scale
    ).reshape(row_count, model_width)
    d_keys = (
        jnp.einsum("hij,ihe->jhe", ds_b, query_heads, preferred_element_type=jnp.float32)
        * score_scale
    ).reshape(key_count, model_width)
    d_values = jnp.einsum(
        "hij,ihe->jhe", probs_b, att_heads, preferred_element_type=jnp.float32
    ).reshape(key_count, model_width)
    near_part = back_project(d_query, w_query) + back_project(d_gate_pre, w_gate)
    summed, bias_grad = reduce(
        jnp.concatenate([d_keys, d_values], axis=1).astype(jnp.bfloat16), ds_b, rows, cols
    )
    key_grad, value_grad = summed[:, :model_width], summed[:, model_width:]
    far_part = back_project(key_grad, w_key) + back_project(value_grad, w_value)
    d_normed = near_part + far_part
    grad_acts = norm_backward(standard, inv_std, norm_gain, d_normed).astype(jnp.bfloat16)
    grad_pair = pair_backward(pair_feats, pair_gain, w_pair, bias_grad)
    return (block_out[None], grad_acts[None], grad_pair)


def solution(mesh):
    placed = (
        P("col", "row", None),
        P("row", "col", None),
        P("row", "col"),
        P(),
        P(),
        P(),
        P(),
        P(),
        P(),
        P(),
        P(),
        P(),
        P(),
        P("col", "row", None),
    )
    return jax.shard_map(
        functools.partial(body, mesh.shape["row"], mesh.shape["col"]),
        mesh=mesh,
        in_specs=placed,
        out_specs=(P("col", "row", None), P("col", "row", None), P("row", "col", None)),
        check_vma=False,
    )
```

profile of v0, /device:TPU:14, one launch (start us, length us, event | category | flops | bytes accessed | tf_op | source)
XLA Modules:
  0.0 251.4 jit_solution(1599680974110057392)
XLA Ops:
  1.7 1.0 convert_reduce_fusion
  2.7 1.1 fusion.32
  4.7 1.0 compare_or_fusion
  5.7 1.8 convolution_convert_fusion.2
  7.5 1.8 convolution_convert_fusion.1
  10.6 1.7 fusion.14
  12.3 2.3 multiply_convert_fusion.2
  15.4 3.4 %copy-done.2 = bf16[128,256,128]{2,1,0:T(8,128)(2,1)S(1)} copy-done((bf16[128,256,128]{2,1,0:T(8,128)(2,1)S(1)}, bf16[128,256,128]{2,1,0:T(8,128)(2,1)}, u32[]{:S(2)}) %copy-start.2) | copy-done | bytes 8388632
  18.8 42.3 %shard_map.157 = bf16[128,16,256]{2,1,0:T(8,128)(2,1)S(1)} custom-call(bf16[128,256,128]{2,1,0:T(8,128)(2,1)S(1)} %copy-done.2, bf16[128,128]{1,0:T(8,128)(2,1)S(1)} %add_convert_fusion.centre, bf16[256,128]{1,0:T(8,128)(2,1)S(1)} %broadcast_8_ones.2.ones, f32[1,128]{1,0:T(1,128)S(1)} %bitcast.106, bf16[16,128]{1,0:T(8,128)(2,1)S(1)} %bitcast.105), custom_call_target="tpu_custom_call" | custom-call | tf_op jit(solution)/shard_map/pallas_call | solution.py:440
  61.5 38.9 %shard_map.158 = (bf16[8,128,1536]{2,1,0:T(8,128)(2,1)S(1)}, bf16[16,128,1024]{2,1,0:T(8,128)(2,1)}) custom-call(bf16[128,1536]{1,0:T(8,128)(2,1)S(1)} %pad_maximum_fusion.1.kv, bf16[16,128,256]{2,1,0:T(8,128)(2,1)S(1)} %fusion.19.tile), custom_call_target="tpu_custom_call" | custom-call | tf_op jit(solution)/shard_map/pallas_call | solution.py:190
  100.4 2.0 fusion.54
  102.3 1.7 copy.31
  104.0 3.2 %copy.29 = bf16[1024,768]{0,1:T(8,128)(2,1)} copy(bf16[1024,768]{1,0:T(8,128)(2,1)} %get-tuple-element.14) | data formatting | bytes 3145728 | tf_op jit(solution)/shard_map/slice | solution.py:514
  107.2 8.8 %fusion.55 = (f32[16,128]{1,0:T(8,128)S(1)}, f32[16,128,1024]{2,1,0:T(8,128)}) fusion(bf16[16,128,1024]{2,1,0:T(8,128)(2,1)} %get-tuple-element.8, bf16[128,16,48]{0,2,1:T(8,128)(2,1)} %bitcast.120, bf16[1024,16,48]{0,2,1:T(8,128)(2,1)S(1)} %bitcast.111), kind=kOutput, calls=%fused_computation.84 | convolution fusion | flops 211813376 | bytes 14360576 | tf_op jit(solution)/shard_map/sub | solution.py:522
  116.0 6.5 %fusion.5 = f32[16,48,128]{2,1,0:T(8,128)} fusion(bf16[1024,16,48]{0,2,1:T(8,128)(2,1)} %bitcast.116, f32[16,128]{1,0:T(8,128)S(1)} %get-tuple-element.17, bf16[16,128,1024]{2,1,0:T(8,128)(2,1)} %get-tuple-element.8, bf16[128,16,48]{0,2,1:T(8,128)(2,1)} %bitcast.121, bf16[1024,16,48]{0,2,1:T(8,128)(2,1)S(1)} %bitcast.112), kind=kOutput, calls=%fused_computation.13 | convolution fusion | flops 415239168 | bytes 7938048 | tf_op jit(solution)/shard_map/hij,jhe->ihe/dot_general | solution.py:524
  122.6 6.8 %fusion.7 = bf16[16,48,1024]{2,1,0:T(8,128)(2,1)} fusion(bf16[128,16,48]{0,2,1:T(8,128)(2,1)} %bitcast.125, f32[16,128]{1,0:T(8,128)S(1)} %get-tuple-element.17, bf16[16,128,1024]{2,1,0:T(8,128)(2,1)} %get-tuple-element.8, bf16[128,16,48]{0,2,1:T(8,128)(2,1)} %bitcast.122, bf16[1024,16,48]{0,2,1:T(8,128)(2,1)S(1)} %bitcast.113), kind=kOutput, calls=%fused_computation.15 | convolution fusion | flops 416025600 | bytes 7741440 | tf_op jit(solution)/shard_map/hij,ihe->jhe/dot_general | solution.py:545
  129.4 1.8 copy.39
  131.2 1.9 copy.36
  133.2 1.2 copy.32
  134.3 1.0 fusion.18
  135.4 5.9 %multiply_reduce_fusion = (f32[16,128]{1,0:T(8,128)S(1)}, f32[16,128,1024]{2,1,0:T(8,128)S(1)}) fusion(f32[16,128,1024]{2,1,0:T(8,128)} %get-tuple-element.18, f32[16,128]{1,0:T(8,128)S(1)} %get-tuple-element.17, bf16[128,16,48]{0,2,1:T(8,128)(2,1)} %bitcast.126, bf16[1024,16,48]{0,2,1:T(8,128)(2,1)} %bitcast.117), kind=kOutput, calls=%fused_computation.2 | convolution fusion | flops 207616000 | bytes 18563072 | tf_op jit(solution)/shard_map/ihe,jhe->hij/dot_general | solution.py:533
  141.3 1.4 multiply_convert_fusion.ds
  142.8 1.6 convolution_multiply_fusion
  144.9 1.4 fusion.56
  146.3 1.3 convolution_add_fusion.2
  148.8 1.9 copy.35
  150.6 3.8 %pad_maximum_fusion.dkv = bf16[8,128,1536]{2,1,0:T(8,128)(2,1)} fusion(bf16[8,128,768]{2,1,0:T(8,128)(2,1)} %copy.36, bf16[8,128,768]{2,1,0:T(8,128)(2,1)} %copy.35), kind=kLoop, calls=%fused_computation.8 | loop fusion | flops 6291456 | bytes 6291456 | tf_op jit(solution)/shard_map/concatenate | solution.py:550
  154.4 60.5 %shard_map.159 = (f32[128,1536]{1,0:T(8,128)S(1)}, f32[16,128,256]{2,1,0:T(8,128)}) custom-call(bf16[8,128,1536]{2,1,0:T(8,128)(2,1)} %pad_maximum_fusion.dkv, bf16[16,128,1024]{2,1,0:T(8,128)(2,1)} %copy-done.5), custom_call_target="tpu_custom_call" | custom-call | tf_op jit(solution)/shard_map/pallas_call | solution.py:378
  215.0 3.0 %copy.44 = f32[16,128,256]{2,0,1:T(8,128)S(1)} copy(f32[16,128,256]{2,1,0:T(8,128)} %get-tuple-element.10) | data formatting | bytes 4194304 | tf_op jit(solution)/shard_map/pallas_call | solution.py:378
  218.0 1.3 fusion.34
  219.2 1.4 fusion.53
  221.5 29.9 %shard_map.160 = bf16[128,256,128]{2,1,0:T(8,128)(2,1)} custom-call(bf16[128,256,128]{2,1,0:T(8,128)(2,1)S(1)} %bitcast.102, bf16[128,128]{1,0:T(8,128)(2,1)S(1)} %add_convert_fusion.centre, bf16[256,128]{1,0:T(8,128)(2,1)S(1)} %broadcast_8_ones.2.ones, f32[128,16,256]{2,1,0:T(8,128)S(1)} %bitcast.103, bf16[64,128]{1,0:T(8,128)(2,1)S(1)} %pad_maximum_fusion.2.weights), custom_call_target="tpu_custom_call" | custom-call | tf_op jit(solution)/shard_map/pallas_call | solution.py:440
  (66 shorter events, 6.9 us)
Async XLA Ops:
  0.6 11.6 %copy-start = (bf16[768,768]{1,0:T(8,128)(2,1)S(1)}, bf16[768,768]{1,0:T(8,128)(2,1)}, u32[]{:S(2)}) copy-start(bf16[768,768]{1,0:T(8,128)(2,1)} %param.24) | copy-start | bytes 3538948
  0.6 8.7 %copy-start.8 = (bf16[1,128,768]{2,1,0:T(8,128)(2,1)S(1)}, bf16[1,128,768]{2,1,0:T(8,128)(2,1)}, u32[]{:S(2)}) copy-start(bf16[1,128,768]{2,1,0:T(8,128)(2,1)} %param.14) | copy-start | bytes 589828
  0.7 8.7 %copy-start.16 = (f32[768]{0:T(1024)S(1)}, f32[768]{0:T(1024)}, u32[]{:S(2)}) copy-start(f32[768]{0:T(1024)} %param.17) | copy-start | bytes 9220
  0.7 8.7 %copy-start.18 = (f32[768]{0:T(1024)S(1)}, f32[768]{0:T(1024)}, u32[]{:S(2)}) copy-start(f32[768]{0:T(1024)} %param.18) | copy-start | bytes 9220
  0.7 8.7 %copy-start.12 = (bf16[768,768]{1,0:T(8,128)(2,1)S(1)}, bf16[768,768]{1,0:T(8,128)(2,1)}, u32[]{:S(2)}) copy-start(bf16[768,768]{1,0:T(8,128)(2,1)} %param.19) | copy-start | bytes 3538948
  0.7 8.7 %copy-start.17 = (f32[768]{0:T(1024)S(1)}, f32[768]{0:T(1024)}, u32[]{:S(2)}) copy-start(f32[768]{0:T(1024)} %param.20) | copy-start | bytes 9220
  9.8 5.6 %copy-start.3 = (bf16[128,16]{0,1:T(8,128)(2,1)S(1)}, bf16[128,16]{0,1:T(8,128)(2,1)}, u32[]{:S(2)}) copy-start(bf16[128,16]{0,1:T(8,128)(2,1)} %param.26) | copy-start | bytes 12292
  9.8 5.6 %copy-start.4 = (f32[128]{0:T(128)S(1)}, f32[128]{0:T(128)}, u32[]{:S(2)}) copy-start(f32[128]{0:T(128)} %param.25) | copy-start | bytes 1540
  15.4 3.4 %copy-start.2 = (bf16[128,256,128]{2,1,0:T(8,128)(2,1)S(1)}, bf16[128,256,128]{2,1,0:T(8,128)(2,1)}, u32[]{:S(2)}) copy-start(bf16[128,256,128]{2,1,0:T(8,128)(2,1)} %feats.3) | copy-start | bytes 25165828
  104.0 18.5 %copy-start.6 = (bf16[1024,768]{0,1:T(8,128)(2,1)}, bf16[1024,768]{0,1:T(8,128)(2,1)S(1)}, u32[]{:S(2)}) copy-start(bf16[1024,768]{0,1:T(8,128)(2,1)S(1)} %copy.31) | copy-start | bytes 4718596
  134.3 6.9 %slice-start.2 = ((s8[8388608]{0:T(1024)(128)(4,1)}), s8[4194304]{0:T(1024)(128)(4,1)S(1)}, s32[]{:S(2)}) async-start(s8[8388608]{0:T(1024)(128)(4,1)} %bitcast.107), calls=%async_computation.2 | async-start | bytes 8388608
  135.4 5.9 %slice-start.3 = ((s8[8388608]{0:T(1024)(128)(4,1)}), s8[4194304]{0:T(1024)(128)(4,1)S(1)}, s32[]{:S(2)}) async-start(s8[8388608]{0:T(1024)(128)(4,1)} %bitcast.107), calls=%async_computation.3 | async-start | bytes 8388608
  141.3 1.4 copy-start.7
  142.7 4.8 %copy-start.5 = (bf16[16,128,1024]{2,1,0:T(8,128)(2,1)}, bf16[16,128,1024]{2,1,0:T(8,128)(2,1)S(1)}, u32[]{:S(2)}) copy-start(bf16[16,128,1024]{2,1,0:T(8,128)(2,1)S(1)} %multiply_convert_fusion.ds) | copy-start | bytes 12582916
  142.7 2.1 copy-start.13
  142.7 3.5 %copy-start.9 = (f32[128,768]{1,0:T(8,128)S(1)}, f32[128,768]{1,0:T(8,128)}, u32[]{:S(2)}) copy-start(f32[128,768]{1,0:T(8,128)} %get-tuple-element.20) | copy-start | bytes 1179652
  142.8 3.5 %copy-start.10 = (bf16[768,768]{1,0:T(8,128)(2,1)S(1)}, bf16[768,768]{1,0:T(8,128)(2,1)}, u32[]{:S(2)}) copy-start(bf16[768,768]{1,0:T(8,128)(2,1)} %param.23) | copy-start | bytes 3538948
  144.3 3.2 %copy-start.15 = (bf16[128,768]{0,1:T(8,128)(2,1)S(1)}, bf16[128,768]{0,1:T(8,128)(2,1)}, u32[]{:S(2)}) copy-start(bf16[128,768]{0,1:T(8,128)(2,1)} %copy.30) | copy-start | bytes 589828
  154.4 67.1 %slice-start = ((s8[8388608]{0:T(1024)(128)(4,1)}), s8[4194304]{0:T(1024)(128)(4,1)S(1)}, s32[]{:S(2)}) async-start(s8[8388608]{0:T(1024)(128)(4,1)} %bitcast.101), calls=%async_computation | async-start | bytes 8388608
  215.0 3.0 %copy-start.14 = (bf16[768,768]{1,0:T(8,128)(2,1)S(1)}, bf16[768,768]{1,0:T(8,128)(2,1)}, u32[]{:S(2)}) copy-start(bf16[768,768]{1,0:T(8,128)(2,1)} %param.21) | copy-start | bytes 3538948
  215.0 4.3 %copy-start.11 = (bf16[768,768]{1,0:T(8,128)(2,1)S(1)}, bf16[768,768]{1,0:T(8,128)(2,1)}, u32[]{:S(2)}) copy-start(bf16[768,768]{1,0:T(8,128)(2,1)} %param.22) | copy-start | bytes 3538948
  215.0 6.5 %slice-start.1 = ((s8[8388608]{0:T(1024)(128)(4,1)}), s8[4194304]{0:T(1024)(128)(4,1)S(1)}, s32[]{:S(2)}) async-start(s8[8388608]{0:T(1024)(128)(4,1)} %bitcast.101), calls=%async_computation.1 | async-start | bytes 8388608
  221.5 29.9 %copy-start.1 = (bf16[768,768]{1,0:T(8,128)(2,1)S(1)}, bf16[768,768]{1,0:T(8,128)(2,1)}, u32[]{:S(2)}) copy-start(bf16[768,768]{1,0:T(8,128)(2,1)} %param.24) | copy-start | bytes 3538948
where the time goes:
time: 252 us; the launch traced here: 251 us
  Pallas kernels  172 us (68%)
  matrix products  44.6 us (18%)
  local copies, waits for them, and re-layouts  22.7 us (9%)
  other arithmetic  11.3 us (4%)
    pallas_call x2, Pallas kernels, pair_call(): pl.pallas_call(kernel, grid=(rows // block,), out_shape=jax.ShapeDtypeStr...  72.2 us
    pallas_call x1, Pallas kernels, reduce(): pl.pallas_call(functools.partial(reduce_kernel, lines, chips), out_shape=...  60.5 us
    pallas_call x1, Pallas kernels, gather(): pl.pallas_call(functools.partial(gather_kernel, lines, chips), out_shape=...  38.9 us
    sub x1, matrix products, body(): attn_probs = jax.nn.softmax(scores, axis=-1)  8.82 us
    slice x3, local copies, waits for them, and re-layouts, body(): all_keys, all_values = (both[:, :model_width], both[:, model_width:])  6.84 us
    dot_general x1, matrix products, body(): jnp.einsum('hij,ihe->jhe', probs_b, att_heads, preferred_element_type=jnp...  6.83 us
    dot_general x1, matrix products, body(): jnp.einsum('hij,jhe->ihe', probs_b, value_heads, preferred_element_type=j...  6.51 us
    unnamed x48, local copies, waits for them, and re-layouts  6.34 us

commit v1 on v0

--- a/solution.py
+++ b/solution.py
@@ -410,27 +410,30 @@
 
 
 def pair_forward_kernel(feats, centre, ones, gain, weights, out):
+    total = None
     for item in range(feats.shape[0]):
         standard, _ = pair_standard(feats[item], centre[...], ones[...])
         normed = (standard * gain[...]).astype(jnp.bfloat16)
-        out[item] = lax.dot_general(
-            weights[...], normed, (((1,), (1,)), ((), ())), preferred_element_type=jnp.float32
-        ).astype(jnp.bfloat16)
-
-
-def pair_backward_kernel(feats, centre, ones, bias_grad, weights, out):
-    for item in range(feats.shape[0]):
+        part = jnp.dot(normed, weights[item], preferred_element_type=jnp.float32)
+        total = part if total is None else total + part
+    out[...] = total.T.reshape(out.shape).astype(jnp.bfloat16)
+
+
+def pair_backward_kernel(feats, centre, ones, bias_grad, high_weights, low_weights, out):
+    block, heads, width = bias_grad.shape
+    grad = bias_grad[...].reshape(block * heads, width).T
+    high = grad.astype(jnp.bfloat16)
+    low = (grad - high.astype(jnp.float32)).astype(jnp.bfloat16)
+    parts = jnp.concatenate([high, low], axis=1)
+    for item in range(block):
         standard, inv_std = pair_standard(feats[item], centre[...], ones[...])
-        grad = bias_grad[item]
-        high = grad.astype(jnp.bfloat16).astype(jnp.float32)
-        low = grad - high
-        parts = jnp.concatenate([high, low, high, low], axis=0).T.astype(jnp.bfloat16)
-        scaled = jnp.dot(parts, weights[...], preferred_element_type=jnp.float32)
+        scaled = jnp.dot(parts, high_weights[item], preferred_element_type=jnp.float32)
+        scaled += jnp.dot(parts, low_weights[item], preferred_element_type=jnp.float32)
         cross_mean = lane_mean(scaled * standard, ones[...])
         out[item] = ((scaled - standard * cross_mean) * inv_std).astype(jnp.bfloat16)
 
 
-def pair_call(kernel, pair_feats, extra, extra_specs, out_shape, block=8):
+def pair_call(kernel, pair_feats, extra, extra_specs, out_shape, block):
     rows, width, channels = pair_feats.shape
     eye = jnp.eye(channels, dtype=jnp.float32)
     centre = (eye - 1.0 / channels).astype(jnp.bfloat16)
@@ -450,23 +453,37 @@
     )(pair_feats, centre, ones, *extra)
 
 
+def spread(matrix, block, axis):
+    picks = jnp.eye(block, dtype=matrix.dtype)
+    if axis == 1:
+        full = picks[:, None, :, None] * matrix[None, :, None, :]
+        return full.reshape(block, matrix.shape[0], block * matrix.shape[1])
+    full = picks[:, :, None, None] * matrix[None, None]
+    full = full.reshape(block, block * matrix.shape[0], matrix.shape[1])
+    return jnp.concatenate([full, full], axis=1)
+
+
 def pair_forward(pair_feats, pair_gain, w_pair):
     rows, width, channels = pair_feats.shape
+    heads = w_pair.shape[1]
+    block = 128 // heads
     return pair_call(
-        pair_forward_kernel, pair_feats, (pair_gain[None], w_pair.T), (False, False),
-        (rows, w_pair.shape[1], width),
+        pair_forward_kernel, pair_feats, (pair_gain[None], spread(w_pair, block, 1)),
+        (False, False), (rows, heads, width), block,
     )
 
 
 def pair_backward(pair_feats, pair_gain, w_pair, bias_grad):
+    block = 128 // w_pair.shape[1]
     scaled = w_pair.astype(jnp.float32).T * pair_gain
     scaled = scaled - jnp.mean(scaled, axis=1, keepdims=True)
     high = lax.reduce_precision(scaled, 8, 7)
-    low = scaled - high
-    weights = jnp.concatenate([high, high, low, low], axis=0).astype(jnp.bfloat16)
+    low = (scaled - high).astype(jnp.bfloat16)
+    high = high.astype(jnp.bfloat16)
     return pair_call(
-        pair_backward_kernel, pair_feats, (jnp.transpose(bias_grad, (1, 0, 2)), weights),
-        (True, False), pair_feats.shape,
+        pair_backward_kernel, pair_feats,
+        (jnp.transpose(bias_grad, (1, 0, 2)), spread(high, block, 0), spread(low, block, 0)),
+        (True, False, False), pair_feats.shape, block,
     )
 
 

time: 252 us -> 246 us (0.976)
  Pallas kernels: 172 us -> 160 us
  local copies, waits for them, and re-layouts: 22.7 us -> 27.7 us
    pallas_call x2, Pallas kernels: 72.2 us -> 60.1 us  [pair_call(): pl.pallas_call(kernel, grid=(rows // block,), out_shape=jax.ShapeDtypeStr...]
    unnamed x48 -> x46, local copies, waits for them, and re-layouts: 6.34 us -> 8.69 us
where the time goes in v1:
time: 246 us; the launch traced here: 245 us
  Pallas kernels  160 us (65%)
  matrix products  44.8 us (18%)
  local copies, waits for them, and re-layouts  27.7 us (11%)
  other arithmetic  11.8 us (5%)
    pallas_call x1, Pallas kernels, reduce(): pl.pallas_call(functools.partial(reduce_kernel, lines, chips), out_shape=...  60.6 us
    pallas_call x2, Pallas kernels, pair_call(): pl.pallas_call(kernel, grid=(rows // block,), out_shape=jax.ShapeDtypeStr...  60.1 us
    pallas_call x1, Pallas kernels, gather(): pl.pallas_call(functools.partial(gather_kernel, lines, chips), out_shape=...  38.9 us
    sub x1, matrix products, body(): attn_probs = jax.nn.softmax(scores, axis=-1)  9.17 us
    unnamed x46, local copies, waits for them, and re-layouts  8.69 us
    slice x3, local copies, waits for them, and re-layouts, body(): all_keys, all_values = (both[:, :model_width], both[:, model_width:])  7.14 us
    dot_general x1, matrix products, body(): jnp.einsum('hij,ihe->jhe', probs_b, att_heads, preferred_element_type=jnp...  7.11 us
    dot_general x1, matrix products, body(): jnp.einsum('hij,jhe->ihe', probs_b, value_heads, preferred_element_type=j...  6.92 us

profile of v1, /device:TPU:14, one launch (start us, length us, event | category | flops | bytes accessed | tf_op | source)
XLA Modules:
  0.0 245.0 jit_solution(1195151555074968346)
XLA Ops:
  1.6 1.0 convert_reduce_fusion
  2.7 1.1 fusion.32
  6.6 1.9 convolution_convert_fusion.2
  8.5 1.8 convolution_convert_fusion.1
  11.0 1.7 fusion.14
  12.7 1.3 multiply_convert_fusion.2
  15.4 3.4 %copy-done.2 = bf16[128,256,128]{2,1,0:T(8,128)(2,1)S(1)} copy-done((bf16[128,256,128]{2,1,0:T(8,128)(2,1)S(1)}, bf16[128,256,128]{2,1,0:T(8,128)(2,1)}, u32[]{:S(2)}) %copy-start.2) | copy-done | bytes 8388632
  18.8 20.9 %shard_map.157 = bf16[128,16,256]{2,1,0:T(8,128)(2,1)S(1)} custom-call(bf16[128,256,128]{2,1,0:T(8,128)(2,1)S(1)} %copy-done.2, bf16[128,128]{1,0:T(8,128)(2,1)S(1)} %add_convert_fusion.centre, bf16[256,128]{1,0:T(8,128)(2,1)S(1)} %broadcast_8_ones.2.ones, f32[1,128]{1,0:T(1,128)S(1)} %bitcast.107, bf16[8,128,128]{2,1,0:T(8,128)(2,1)S(1)} %get-tuple-element.19.weights), custom_call_target="tpu_custom_call" | custom-call | tf_op jit(solution)/shard_map/pallas_call | solution.py:443
  40.0 38.9 %shard_map.158 = (bf16[8,128,1536]{2,1,0:T(8,128)(2,1)S(1)}, bf16[16,128,1024]{2,1,0:T(8,128)(2,1)}) custom-call(bf16[128,1536]{1,0:T(8,128)(2,1)S(1)} %pad_maximum_fusion.3.kv, bf16[16,128,256]{2,1,0:T(8,128)(2,1)S(1)} %fusion.19.tile), custom_call_target="tpu_custom_call" | custom-call | tf_op jit(solution)/shard_map/pallas_call | solution.py:190
  79.0 2.0 fusion.55
  80.9 2.6 %copy.33 = bf16[1024,768]{0,1:T(8,128)(2,1)} copy(bf16[1024,768]{1,0:T(8,128)(2,1)} %get-tuple-element.13) | data formatting | bytes 3145728 | tf_op jit(solution)/shard_map/slice | solution.py:531
  83.5 2.6 %copy.31 = bf16[1024,768]{0,1:T(8,128)(2,1)} copy(bf16[1024,768]{1,0:T(8,128)(2,1)} %get-tuple-element.14) | data formatting | bytes 3145728 | tf_op jit(solution)/shard_map/slice | solution.py:531
  86.1 9.2 %fusion.56 = (f32[16,128]{1,0:T(8,128)S(1)}, f32[16,128,1024]{2,1,0:T(8,128)}) fusion(bf16[16,128,1024]{2,1,0:T(8,128)(2,1)} %get-tuple-element.8, bf16[128,16,48]{0,2,1:T(8,128)(2,1)S(1)} %bitcast.121, bf16[1024,16,48]{0,2,1:T(8,128)(2,1)} %bitcast.112), kind=kOutput, calls=%fused_computation.90 | convolution fusion | flops 211813376 | bytes 14360576 | tf_op jit(solution)/shard_map/sub | solution.py:539
  95.3 6.9 %fusion.5 = f32[16,48,128]{2,1,0:T(8,128)} fusion(bf16[1024,16,48]{0,2,1:T(8,128)(2,1)} %bitcast.117, f32[16,128]{1,0:T(8,128)S(1)} %get-tuple-element.20, bf16[16,128,1024]{2,1,0:T(8,128)(2,1)} %get-tuple-element.8, bf16[128,16,48]{0,2,1:T(8,128)(2,1)S(1)} %bitcast.122, bf16[1024,16,48]{0,2,1:T(8,128)(2,1)} %bitcast.113), kind=kOutput, calls=%fused_computation.13 | convolution fusion | flops 415239168 | bytes 7938048 | tf_op jit(solution)/shard_map/hij,jhe->ihe/dot_general | solution.py:541
  102.2 7.1 %fusion.7 = bf16[16,48,1024]{2,1,0:T(8,128)(2,1)} fusion(bf16[128,16,48]{0,2,1:T(8,128)(2,1)S(1)} %bitcast.127, f32[16,128]{1,0:T(8,128)S(1)} %get-tuple-element.20, bf16[16,128,1024]{2,1,0:T(8,128)(2,1)} %get-tuple-element.8, bf16[128,16,48]{0,2,1:T(8,128)(2,1)S(1)} %bitcast.123, bf16[1024,16,48]{0,2,1:T(8,128)(2,1)} %bitcast.114), kind=kOutput, calls=%fused_computation.15 | convolution fusion | flops 416025600 | bytes 7741440 | tf_op jit(solution)/shard_map/hij,ihe->jhe/dot_general | solution.py:562
  109.3 3.0 %copy.41 = bf16[96,8,8,128]{3,2,1,0:T(8,128)(2,1)} copy(bf16[96,8,8,128]{3,1,2,0:T(8,128)(2,1)} %bitcast.119) | data formatting | bytes 3145728
  112.3 2.9 %copy.38 = bf16[8,128,768]{2,1,0:T(8,128)(2,1)} copy(bf16[8,128,768]{1,0,2:T(8,128)(2,1)} %bitcast.110) | data formatting | bytes 3145728 | tf_op jit(solution)/shard_map/concatenate | solution.py:567
  115.2 1.2 copy.34
  116.4 1.0 fusion.18
  117.4 5.9 %multiply_reduce_fusion = (f32[16,128]{1,0:T(8,128)S(1)}, f32[16,128,1024]{2,1,0:T(8,128)S(1)}) fusion(f32[16,128,1024]{2,1,0:T(8,128)} %get-tuple-element.21, f32[16,128]{1,0:T(8,128)S(1)} %get-tuple-element.20, bf16[128,16,48]{0,2,1:T(8,128)(2,1)} %bitcast.126, bf16[1024,16,48]{0,2,1:T(8,128)(2,1)} %bitcast.118), kind=kOutput, calls=%fused_computation.2 | convolution fusion | flops 207616000 | bytes 18563072 | tf_op jit(solution)/shard_map/ihe,jhe->hij/dot_general | solution.py:550
  123.4 1.4 multiply_convert_fusion.ds
  124.8 1.6 convolution_multiply_fusion
  126.9 1.4 fusion.57
  128.4 1.3 convolution_add_fusion.2
  130.4 1.6 copy.40
  132.0 2.9 %copy.37 = bf16[8,128,768]{2,1,0:T(8,128)(2,1)} copy(bf16[8,128,768]{1,0,2:T(8,128)(2,1)} %bitcast.111) | data formatting | bytes 3145728 | tf_op jit(solution)/shard_map/concatenate | solution.py:567
  134.9 3.8 %pad_maximum_fusion.dkv = bf16[8,128,1536]{2,1,0:T(8,128)(2,1)} fusion(bf16[8,128,768]{2,1,0:T(8,128)(2,1)} %copy.38, bf16[8,128,768]{2,1,0:T(8,128)(2,1)} %copy.37), kind=kLoop, calls=%fused_computation.8 | loop fusion | flops 6291456 | bytes 6291456 | tf_op jit(solution)/shard_map/concatenate | solution.py:567
  138.7 60.6 %shard_map.159 = (f32[128,1536]{1,0:T(8,128)S(1)}, f32[16,128,256]{2,1,0:T(8,128)}) custom-call(bf16[8,128,1536]{2,1,0:T(8,128)(2,1)} %pad_maximum_fusion.dkv, bf16[16,128,1024]{2,1,0:T(8,128)(2,1)} %copy-done.4), custom_call_target="tpu_custom_call" | custom-call | tf_op jit(solution)/shard_map/pallas_call | solution.py:378
  199.3 3.0 %copy.46 = f32[16,128,256]{2,0,1:T(8,128)S(1)} copy(f32[16,128,256]{2,1,0:T(8,128)} %get-tuple-element.10) | data formatting | bytes 4194304 | tf_op jit(solution)/shard_map/pallas_call | solution.py:378
  202.2 1.3 fusion.34
  203.5 1.4 fusion.54
  205.8 39.2 %shard_map.160 = bf16[128,256,128]{2,1,0:T(8,128)(2,1)} custom-call(bf16[128,256,128]{2,1,0:T(8,128)(2,1)S(1)} %bitcast.104, bf16[128,128]{1,0:T(8,128)(2,1)S(1)} %add_convert_fusion.centre, bf16[256,128]{1,0:T(8,128)(2,1)S(1)} %broadcast_8_ones.2.ones, f32[128,16,256]{2,1,0:T(8,128)S(1)} %bitcast.105, ...), custom_call_target="tpu_custom_call" | custom-call | tf_op jit(solution)/shard_map/pallas_call | solution.py:443
  (72 shorter events, 8.2 us)
Async XLA Ops:
  0.6 12.0 %copy-start = (bf16[768,768]{1,0:T(8,128)(2,1)S(1)}, bf16[768,768]{1,0:T(8,128)(2,1)}, u32[]{:S(2)}) copy-start(bf16[768,768]{1,0:T(8,128)(2,1)} %param.24) | copy-start | bytes 3538948
  0.6 9.7 %copy-start.6 = (bf16[1,128,768]{2,1,0:T(8,128)(2,1)S(1)}, bf16[1,128,768]{2,1,0:T(8,128)(2,1)}, u32[]{:S(2)}) copy-start(bf16[1,128,768]{2,1,0:T(8,128)(2,1)} %param.14) | copy-start | bytes 589828
  0.7 9.7 %copy-start.15 = (f32[768]{0:T(1024)S(1)}, f32[768]{0:T(1024)}, u32[]{:S(2)}) copy-start(f32[768]{0:T(1024)} %param.17) | copy-start | bytes 9220
  0.7 9.7 %copy-start.17 = (f32[768]{0:T(1024)S(1)}, f32[768]{0:T(1024)}, u32[]{:S(2)}) copy-start(f32[768]{0:T(1024)} %param.18) | copy-start | bytes 9220
  0.7 9.7 %copy-start.16 = (f32[768]{0:T(1024)S(1)}, f32[768]{0:T(1024)}, u32[]{:S(2)}) copy-start(f32[768]{0:T(1024)} %param.20) | copy-start | bytes 9220
  6.6 3.8 %copy-start.10 = (bf16[768,768]{1,0:T(8,128)(2,1)S(1)}, bf16[768,768]{1,0:T(8,128)(2,1)}, u32[]{:S(2)}) copy-start(bf16[768,768]{1,0:T(8,128)(2,1)} %param.19) | copy-start | bytes 3538948
  10.3 2.4 copy-start.13
  12.7 2.7 %copy-start.3 = (f32[128]{0:T(128)S(1)}, f32[128]{0:T(128)}, u32[]{:S(2)}) copy-start(f32[128]{0:T(128)} %param.25) | copy-start | bytes 1540
  15.4 3.4 %copy-start.2 = (bf16[128,256,128]{2,1,0:T(8,128)(2,1)S(1)}, bf16[128,256,128]{2,1,0:T(8,128)(2,1)}, u32[]{:S(2)}) copy-start(bf16[128,256,128]{2,1,0:T(8,128)(2,1)} %feats.3) | copy-start | bytes 25165828
  95.3 6.9 %copy-start.14 = (bf16[128,768]{0,1:T(8,128)(2,1)S(1)}, bf16[128,768]{0,1:T(8,128)(2,1)}, u32[]{:S(2)}) copy-start(bf16[128,768]{0,1:T(8,128)(2,1)} %copy.35) | copy-start | bytes 589828
  116.4 6.9 %slice-start.2 = ((s8[8388608]{0:T(1024)(128)(4,1)}), s8[4194304]{0:T(1024)(128)(4,1)S(1)}, s32[]{:S(2)}) async-start(s8[8388608]{0:T(1024)(128)(4,1)} %bitcast.108), calls=%async_computation.2 | async-start | bytes 8388608
  117.4 5.9 %slice-start.3 = ((s8[8388608]{0:T(1024)(128)(4,1)}), s8[4194304]{0:T(1024)(128)(4,1)S(1)}, s32[]{:S(2)}) async-start(s8[8388608]{0:T(1024)(128)(4,1)} %bitcast.108), calls=%async_computation.3 | async-start | bytes 8388608
  123.3 1.4 copy-start.5
  124.8 4.9 %copy-start.4 = (bf16[16,128,1024]{2,1,0:T(8,128)(2,1)}, bf16[16,128,1024]{2,1,0:T(8,128)(2,1)S(1)}, u32[]{:S(2)}) copy-start(bf16[16,128,1024]{2,1,0:T(8,128)(2,1)S(1)} %multiply_convert_fusion.ds) | copy-start | bytes 12582916
  124.8 2.1 copy-start.11
  124.8 3.5 %copy-start.7 = (f32[128,768]{1,0:T(8,128)S(1)}, f32[128,768]{1,0:T(8,128)}, u32[]{:S(2)}) copy-start(f32[128,768]{1,0:T(8,128)} %get-tuple-element.23) | copy-start | bytes 1179652
  124.8 3.5 %copy-start.8 = (bf16[768,768]{1,0:T(8,128)(2,1)S(1)}, bf16[768,768]{1,0:T(8,128)(2,1)}, u32[]{:S(2)}) copy-start(bf16[768,768]{1,0:T(8,128)(2,1)} %param.23) | copy-start | bytes 3538948
  138.7 67.1 %slice-start = ((s8[8388608]{0:T(1024)(128)(4,1)}), s8[4194304]{0:T(1024)(128)(4,1)S(1)}, s32[]{:S(2)}) async-start(s8[8388608]{0:T(1024)(128)(4,1)} %bitcast.103), calls=%async_computation | async-start | bytes 8388608
  199.2 3.0 %copy-start.12 = (bf16[768,768]{1,0:T(8,128)(2,1)S(1)}, bf16[768,768]{1,0:T(8,128)(2,1)}, u32[]{:S(2)}) copy-start(bf16[768,768]{1,0:T(8,128)(2,1)} %param.21) | copy-start | bytes 3538948
  199.2 4.3 %copy-start.9 = (bf16[768,768]{1,0:T(8,128)(2,1)S(1)}, bf16[768,768]{1,0:T(8,128)(2,1)}, u32[]{:S(2)}) copy-start(bf16[768,768]{1,0:T(8,128)(2,1)} %param.22) | copy-start | bytes 3538948
  199.3 6.5 %slice-start.1 = ((s8[8388608]{0:T(1024)(128)(4,1)}), s8[4194304]{0:T(1024)(128)(4,1)S(1)}, s32[]{:S(2)}) async-start(s8[8388608]{0:T(1024)(128)(4,1)} %bitcast.103), calls=%async_computation.1 | async-start | bytes 8388608
  205.8 39.2 %copy-start.1 = (bf16[768,768]{1,0:T(8,128)(2,1)S(1)}, bf16[768,768]{1,0:T(8,128)(2,1)}, u32[]{:S(2)}) copy-start(bf16[768,768]{1,0:T(8,128)(2,1)} %param.24) | copy-start | bytes 3538948

commit v2 on v0

--- a/solution.py
+++ b/solution.py
@@ -410,12 +410,13 @@
 
 
 def pair_forward_kernel(feats, centre, ones, gain, weights, out):
+    total = None
     for item in range(feats.shape[0]):
         standard, _ = pair_standard(feats[item], centre[...], ones[...])
         normed = (standard * gain[...]).astype(jnp.bfloat16)
-        out[item] = lax.dot_general(
-            weights[...], normed, (((1,), (1,)), ((), ())), preferred_element_type=jnp.float32
-        ).astype(jnp.bfloat16)
+        part = jnp.dot(normed, weights[item], preferred_element_type=jnp.float32)
+        total = part if total is None else total + part
+    out[...] = total.T.reshape(out.shape).astype(jnp.bfloat16)
 
 
 def pair_backward_kernel(feats, centre, ones, bias_grad, weights, out):
@@ -430,7 +431,7 @@
         out[item] = ((scaled - standard * cross_mean) * inv_std).astype(jnp.bfloat16)
 
 
-def pair_call(kernel, pair_feats, extra, extra_specs, out_shape, block=8):
+def pair_call(kernel, pair_feats, extra, extra_specs, out_shape, block):
     rows, width, channels = pair_feats.shape
     eye = jnp.eye(channels, dtype=jnp.float32)
     centre = (eye - 1.0 / channels).astype(jnp.bfloat16)
@@ -450,11 +451,19 @@
     )(pair_feats, centre, ones, *extra)
 
 
+def spread(matrix, block):
+    picks = jnp.eye(block, dtype=matrix.dtype)
+    full = picks[:, None, :, None] * matrix[None, :, None, :]
+    return full.reshape(block, matrix.shape[0], block * matrix.shape[1])
+
+
 def pair_forward(pair_feats, pair_gain, w_pair):
     rows, width, channels = pair_feats.shape
+    heads = w_pair.shape[1]
+    block = 128 // heads
     return pair_call(
-        pair_forward_kernel, pair_feats, (pair_gain[None], w_pair.T), (False, False),
-        (rows, w_pair.shape[1], width),
+        pair_forward_kernel, pair_feats, (pair_gain[None], spread(w_pair, block)),
+        (False, False), (rows, heads, width), block,
     )
 
 
@@ -466,7 +475,7 @@
     weights = jnp.concatenate([high, high, low, low], axis=0).astype(jnp.bfloat16)
     return pair_call(
         pair_backward_kernel, pair_feats, (jnp.transpose(bias_grad, (1, 0, 2)), weights),
-        (True, False), pair_feats.shape,
+        (True, False), pair_feats.shape, 8,
     )
 
 

time: 252 us -> 232 us (0.921)
  Pallas kernels: 172 us -> 150 us
    pallas_call x2, Pallas kernels: 72.2 us -> 50.9 us  [pair_call(): pl.pallas_call(kernel, grid=(rows // block,), out_shape=jax.ShapeDtypeStr...]
    unnamed x48 -> x46, local copies, waits for them, and re-layouts: 6.34 us -> 6.33 us
where the time goes in v2:
time: 232 us; the launch traced here: 231 us
  Pallas kernels  150 us (65%)
  matrix products  44.6 us (19%)
  local copies, waits for them, and re-layouts  23.8 us (10%)
  other arithmetic  11.4 us (5%)
    pallas_call x1, Pallas kernels, reduce(): pl.pallas_call(functools.partial(reduce_kernel, lines, chips), out_shape=...  60.6 us
    pallas_call x2, Pallas kernels, pair_call(): pl.pallas_call(kernel, grid=(rows // block,), out_shape=jax.ShapeDtypeStr...  50.9 us
    pallas_call x1, Pallas kernels, gather(): pl.pallas_call(functools.partial(gather_kernel, lines, chips), out_shape=...  38.9 us
    sub x1, matrix products, body(): attn_probs = jax.nn.softmax(scores, axis=-1)  8.82 us
    slice x3, local copies, waits for them, and re-layouts, body(): all_keys, all_values = (both[:, :model_width], both[:, model_width:])  6.85 us
    dot_general x1, matrix products, body(): jnp.einsum('hij,ihe->jhe', probs_b, att_heads, preferred_element_type=jnp...  6.83 us
    dot_general x1, matrix products, body(): jnp.einsum('hij,jhe->ihe', probs_b, value_heads, preferred_element_type=j...  6.53 us
    unnamed x46, local copies, waits for them, and re-layouts  6.33 us

profile of v2, /device:TPU:14, one launch (start us, length us, event | category | flops | bytes accessed | tf_op | source)
XLA Modules:
  0.0 231.3 jit_solution(8243720264365497204)
XLA Ops:
  1.7 1.0 convert_reduce_fusion
  2.7 1.1 fusion.32
  4.8 1.0 compare_or_fusion
  6.7 1.8 convolution_convert_fusion.2
  8.5 1.8 convolution_convert_fusion.1
  11.6 1.7 fusion.14
  13.3 2.3 multiply_convert_fusion.2
  16.4 3.4 %copy-done.2 = bf16[128,256,128]{2,1,0:T(8,128)(2,1)S(1)} copy-done((bf16[128,256,128]{2,1,0:T(8,128)(2,1)S(1)}, bf16[128,256,128]{2,1,0:T(8,128)(2,1)}, u32[]{:S(2)}) %copy-start.2) | copy-done | bytes 8388632
  19.8 21.0 %shard_map.157 = bf16[128,16,256]{2,1,0:T(8,128)(2,1)S(1)} custom-call(bf16[128,256,128]{2,1,0:T(8,128)(2,1)S(1)} %copy-done.2, bf16[128,128]{1,0:T(8,128)(2,1)S(1)} %add_convert_fusion.centre, bf16[256,128]{1,0:T(8,128)(2,1)S(1)} %broadcast_8_ones.2.ones, f32[1,128]{1,0:T(1,128)S(1)} %bitcast.105, bf16[8,128,128]{2,1,0:T(8,128)(2,1)S(1)} %broadcast_multiply_fusion.weights), custom_call_target="tpu_custom_call" | custom-call | tf_op jit(solution)/shard_map/pallas_call | solution.py:441
  41.2 38.9 %shard_map.158 = (bf16[8,128,1536]{2,1,0:T(8,128)(2,1)S(1)}, bf16[16,128,1024]{2,1,0:T(8,128)(2,1)}) custom-call(bf16[128,1536]{1,0:T(8,128)(2,1)S(1)} %pad_maximum_fusion.1.kv, bf16[16,128,256]{2,1,0:T(8,128)(2,1)S(1)} %fusion.19.tile), custom_call_target="tpu_custom_call" | custom-call | tf_op jit(solution)/shard_map/pallas_call | solution.py:190
  80.1 2.0 fusion.55
  82.1 1.7 copy.33
  83.8 3.2 %copy.31 = bf16[1024,768]{0,1:T(8,128)(2,1)} copy(bf16[1024,768]{1,0:T(8,128)(2,1)} %get-tuple-element.14) | data formatting | bytes 3145728 | tf_op jit(solution)/shard_map/slice | solution.py:523
  87.0 8.8 %fusion.56 = (f32[16,128]{1,0:T(8,128)S(1)}, f32[16,128,1024]{2,1,0:T(8,128)}) fusion(bf16[16,128,1024]{2,1,0:T(8,128)(2,1)} %get-tuple-element.8, bf16[128,16,48]{0,2,1:T(8,128)(2,1)} %bitcast.119, bf16[1024,16,48]{0,2,1:T(8,128)(2,1)S(1)} %bitcast.110), kind=kOutput, calls=%fused_computation.87 | convolution fusion | flops 211813376 | bytes 14360576 | tf_op jit(solution)/shard_map/sub | solution.py:531
  95.8 6.5 %fusion.5 = f32[16,48,128]{2,1,0:T(8,128)} fusion(bf16[1024,16,48]{0,2,1:T(8,128)(2,1)} %bitcast.115, f32[16,128]{1,0:T(8,128)S(1)} %get-tuple-element.17, bf16[16,128,1024]{2,1,0:T(8,128)(2,1)} %get-tuple-element.8, bf16[128,16,48]{0,2,1:T(8,128)(2,1)} %bitcast.120, bf16[1024,16,48]{0,2,1:T(8,128)(2,1)S(1)} %bitcast.111), kind=kOutput, calls=%fused_computation.13 | convolution fusion | flops 415239168 | bytes 7938048 | tf_op jit(solution)/shard_map/hij,jhe->ihe/dot_general | solution.py:533
  102.3 6.8 %fusion.7 = bf16[16,48,1024]{2,1,0:T(8,128)(2,1)} fusion(bf16[128,16,48]{0,2,1:T(8,128)(2,1)} %bitcast.124, f32[16,128]{1,0:T(8,128)S(1)} %get-tuple-element.17, bf16[16,128,1024]{2,1,0:T(8,128)(2,1)} %get-tuple-element.8, bf16[128,16,48]{0,2,1:T(8,128)(2,1)} %bitcast.121, bf16[1024,16,48]{0,2,1:T(8,128)(2,1)S(1)} %bitcast.112), kind=kOutput, calls=%fused_computation.15 | convolution fusion | flops 416025600 | bytes 7741440 | tf_op jit(solution)/shard_map/hij,ihe->jhe/dot_general | solution.py:554
  109.2 1.9 copy.41
  111.0 2.0 copy.38
  113.0 1.2 copy.34
  114.2 1.0 fusion.18
  115.2 5.9 %multiply_reduce_fusion = (f32[16,128]{1,0:T(8,128)S(1)}, f32[16,128,1024]{2,1,0:T(8,128)S(1)}) fusion(f32[16,128,1024]{2,1,0:T(8,128)} %get-tuple-element.18, f32[16,128]{1,0:T(8,128)S(1)} %get-tuple-element.17, bf16[128,16,48]{0,2,1:T(8,128)(2,1)} %bitcast.125, bf16[1024,16,48]{0,2,1:T(8,128)(2,1)} %bitcast.116), kind=kOutput, calls=%fused_computation.2 | convolution fusion | flops 207616000 | bytes 18563072 | tf_op jit(solution)/shard_map/ihe,jhe->hij/dot_general | solution.py:542
  121.2 1.4 multiply_convert_fusion.ds
  122.6 1.6 convolution_multiply_fusion
  124.7 1.4 fusion.57
  126.2 1.3 convolution_add_fusion.2
  128.6 1.9 copy.37
  130.5 3.8 %pad_maximum_fusion.dkv = bf16[8,128,1536]{2,1,0:T(8,128)(2,1)} fusion(bf16[8,128,768]{2,1,0:T(8,128)(2,1)} %copy.38, bf16[8,128,768]{2,1,0:T(8,128)(2,1)} %copy.37), kind=kLoop, calls=%fused_computation.8 | loop fusion | flops 6291456 | bytes 6291456 | tf_op jit(solution)/shard_map/concatenate | solution.py:559
  134.3 60.6 %shard_map.159 = (f32[128,1536]{1,0:T(8,128)S(1)}, f32[16,128,256]{2,1,0:T(8,128)}) custom-call(bf16[8,128,1536]{2,1,0:T(8,128)(2,1)} %pad_maximum_fusion.dkv, bf16[16,128,1024]{2,1,0:T(8,128)(2,1)} %copy-done.4), custom_call_target="tpu_custom_call" | custom-call | tf_op jit(solution)/shard_map/pallas_call | solution.py:378
  194.9 3.0 %copy.46 = f32[16,128,256]{2,0,1:T(8,128)S(1)} copy(f32[16,128,256]{2,1,0:T(8,128)} %get-tuple-element.10) | data formatting | bytes 4194304 | tf_op jit(solution)/shard_map/pallas_call | solution.py:378
  197.8 1.3 fusion.34
  199.1 1.4 fusion.54
  201.4 29.9 %shard_map.160 = bf16[128,256,128]{2,1,0:T(8,128)(2,1)} custom-call(bf16[128,256,128]{2,1,0:T(8,128)(2,1)S(1)} %bitcast.102, bf16[128,128]{1,0:T(8,128)(2,1)S(1)} %add_convert_fusion.centre, bf16[256,128]{1,0:T(8,128)(2,1)S(1)} %broadcast_8_ones.2.ones, f32[128,16,256]{2,1,0:T(8,128)S(1)} %bitcast.103, bf16[64,128]{1,0:T(8,128)(2,1)S(1)} %pad_maximum_fusion.2.weights), custom_call_target="tpu_custom_call" | custom-call | tf_op jit(solution)/shard_map/pallas_call | solution.py:441
  (70 shorter events, 7.9 us)
Async XLA Ops:
  0.6 12.7 %copy-start = (bf16[768,768]{1,0:T(8,128)(2,1)S(1)}, bf16[768,768]{1,0:T(8,128)(2,1)}, u32[]{:S(2)}) copy-start(bf16[768,768]{1,0:T(8,128)(2,1)} %param.24) | copy-start | bytes 3538948
  0.6 9.7 %copy-start.7 = (bf16[1,128,768]{2,1,0:T(8,128)(2,1)S(1)}, bf16[1,128,768]{2,1,0:T(8,128)(2,1)}, u32[]{:S(2)}) copy-start(bf16[1,128,768]{2,1,0:T(8,128)(2,1)} %param.14) | copy-start | bytes 589828
  0.7 9.7 %copy-start.15 = (f32[768]{0:T(1024)S(1)}, f32[768]{0:T(1024)}, u32[]{:S(2)}) copy-start(f32[768]{0:T(1024)} %param.17) | copy-start | bytes 9220
  0.7 9.7 %copy-start.17 = (f32[768]{0:T(1024)S(1)}, f32[768]{0:T(1024)}, u32[]{:S(2)}) copy-start(f32[768]{0:T(1024)} %param.18) | copy-start | bytes 9220
  0.7 9.7 %copy-start.11 = (bf16[768,768]{1,0:T(8,128)(2,1)S(1)}, bf16[768,768]{1,0:T(8,128)(2,1)}, u32[]{:S(2)}) copy-start(bf16[768,768]{1,0:T(8,128)(2,1)} %param.19) | copy-start | bytes 3538948
  0.7 9.7 %copy-start.16 = (f32[768]{0:T(1024)S(1)}, f32[768]{0:T(1024)}, u32[]{:S(2)}) copy-start(f32[768]{0:T(1024)} %param.20) | copy-start | bytes 9220
  11.6 4.8 %copy-start.3 = (f32[128]{0:T(128)S(1)}, f32[128]{0:T(128)}, u32[]{:S(2)}) copy-start(f32[128]{0:T(128)} %param.25) | copy-start | bytes 1540
  16.4 3.4 %copy-start.2 = (bf16[128,256,128]{2,1,0:T(8,128)(2,1)S(1)}, bf16[128,256,128]{2,1,0:T(8,128)(2,1)}, u32[]{:S(2)}) copy-start(bf16[128,256,128]{2,1,0:T(8,128)(2,1)} %feats.3) | copy-start | bytes 25165828
  83.8 18.5 %copy-start.5 = (bf16[1024,768]{0,1:T(8,128)(2,1)}, bf16[1024,768]{0,1:T(8,128)(2,1)S(1)}, u32[]{:S(2)}) copy-start(bf16[1024,768]{0,1:T(8,128)(2,1)S(1)} %copy.33) | copy-start | bytes 4718596
  114.2 6.9 %slice-start.2 = ((s8[8388608]{0:T(1024)(128)(4,1)}), s8[4194304]{0:T(1024)(128)(4,1)S(1)}, s32[]{:S(2)}) async-start(s8[8388608]{0:T(1024)(128)(4,1)} %bitcast.106), calls=%async_computation.2 | async-start | bytes 8388608
  115.2 5.9 %slice-start.3 = ((s8[8388608]{0:T(1024)(128)(4,1)}), s8[4194304]{0:T(1024)(128)(4,1)S(1)}, s32[]{:S(2)}) async-start(s8[8388608]{0:T(1024)(128)(4,1)} %bitcast.106), calls=%async_computation.3 | async-start | bytes 8388608
  121.2 1.4 copy-start.6
  122.6 4.8 %copy-start.4 = (bf16[16,128,1024]{2,1,0:T(8,128)(2,1)}, bf16[16,128,1024]{2,1,0:T(8,128)(2,1)S(1)}, u32[]{:S(2)}) copy-start(bf16[16,128,1024]{2,1,0:T(8,128)(2,1)S(1)} %multiply_convert_fusion.ds) | copy-start | bytes 12582916
  122.6 2.1 copy-start.12
  122.6 3.5 %copy-start.8 = (f32[128,768]{1,0:T(8,128)S(1)}, f32[128,768]{1,0:T(8,128)}, u32[]{:S(2)}) copy-start(f32[128,768]{1,0:T(8,128)} %get-tuple-element.20) | copy-start | bytes 1179652
  122.6 3.5 %copy-start.9 = (bf16[768,768]{1,0:T(8,128)(2,1)S(1)}, bf16[768,768]{1,0:T(8,128)(2,1)}, u32[]{:S(2)}) copy-start(bf16[768,768]{1,0:T(8,128)(2,1)} %param.23) | copy-start | bytes 3538948
  124.2 3.2 %copy-start.14 = (bf16[128,768]{0,1:T(8,128)(2,1)S(1)}, bf16[128,768]{0,1:T(8,128)(2,1)}, u32[]{:S(2)}) copy-start(bf16[128,768]{0,1:T(8,128)(2,1)} %copy.32) | copy-start | bytes 589828
  134.3 67.1 %slice-start = ((s8[8388608]{0:T(1024)(128)(4,1)}), s8[4194304]{0:T(1024)(128)(4,1)S(1)}, s32[]{:S(2)}) async-start(s8[8388608]{0:T(1024)(128)(4,1)} %bitcast.101), calls=%async_computation | async-start | bytes 8388608
  194.8 3.0 %copy-start.13 = (bf16[768,768]{1,0:T(8,128)(2,1)S(1)}, bf16[768,768]{1,0:T(8,128)(2,1)}, u32[]{:S(2)}) copy-start(bf16[768,768]{1,0:T(8,128)(2,1)} %param.21) | copy-start | bytes 3538948
  194.8 4.3 %copy-start.10 = (bf16[768,768]{1,0:T(8,128)(2,1)S(1)}, bf16[768,768]{1,0:T(8,128)(2,1)}, u32[]{:S(2)}) copy-start(bf16[768,768]{1,0:T(8,128)(2,1)} %param.22) | copy-start | bytes 3538948
  194.9 6.5 %slice-start.1 = ((s8[8388608]{0:T(1024)(128)(4,1)}), s8[4194304]{0:T(1024)(128)(4,1)S(1)}, s32[]{:S(2)}) async-start(s8[8388608]{0:T(1024)(128)(4,1)} %bitcast.101), calls=%async_computation.1 | async-start | bytes 8388608
  201.4 29.9 %copy-start.1 = (bf16[768,768]{1,0:T(8,128)(2,1)S(1)}, bf16[768,768]{1,0:T(8,128)(2,1)}, u32[]{:S(2)}) copy-start(bf16[768,768]{1,0:T(8,128)(2,1)} %param.24) | copy-start | bytes 3538948
